TPU v7x, 256 devices: a whole 4x4x8 slice. The times are simulated.
256 devices in a mesh: band: 8 (over y, x_lo), slab: 32 (over x_hi, z, core).
Axes of the slice: x: 4 (x_hi: 2, x_lo: 2; x = x_hi * 2 + x_lo), y: 4, z: 8, core: 2. Of those that a mesh axis runs over, the one named last changes fastest.
Arguments:
- wavefunctions: float32 [8, 128, 128, 128], P('band', 'slab'), may hold values from -6 to 6
Outputs:
- exchange_field: float32 [8, 128, 128, 128], P('band', 'slab')
All inputs are finite; a program needn't handle non-finite values.
Results may differ from a plain program's by a relative error of at most 0.0003.
Values sent between devices are 32-bit elements; how exact they have to be, the bound alone decides.
A program may use at most 64 MiB of HBM per device.

v0:
```python
import jax
import jax.numpy as jnp
import ml_dtypes
import numpy as np
from jax import lax
from jax.experimental import pallas as pl
from jax.experimental.pallas import tpu as pltpu
from jax.sharding import PartitionSpec as P

MESH = pl.DeviceIdType.MESH
N = 128
PEERS = 32
USED, PITCH = 18, 24
BF16, F32 = jnp.bfloat16, jnp.float32
FWD, INV, Y_FWD, Y_INV, HALF_FWD, HALF_INV = range(6)

HELD = (0, 1, 3, 4)
ROUTES = (
    ((0, 7), (7, 5), (5, 4)),
    ((0, 1), (0, 6), (6, 5)),
    ((0, 1), (1, 2), (0, 7), (7, 6)),
    ((0, 2), (2, 3), (0, 7)),
    ((0, 1), (1, 3), (3, 4)),
    ((0, 1), (1, 2), (0, 5), (5, 4)),
    ((0, 2), (2, 3), (0, 6), (6, 5)),
    ((0, 3), (3, 4), (0, 7), (7, 6)),
)


def stride_of(start, end):
    return end - start if start <= end <= 4 and start < 4 else end - (start or 8)


def source_core(r):
    return 0 if r in HELD else 1


def place(distance, r):
    if distance == 0:
        return source_core(r), 0
    return (0, distance) if distance < 4 else (1, 7 - distance)


def starts_at(distance, r):
    return [end for start, end in ROUTES[r] if start == distance]


def weight_tables():
    index = np.arange(N)
    angle = 2.0 * np.pi / N * (index[:, None] * index[None, :] % N)
    cos, sin = np.cos(angle), np.sin(angle)
    forward = np.block([[cos, sin], [-sin, cos]])
    sign = 1.0 - 2.0 * (index % 2)
    ones = np.ones(N)

    def order(width):
        peer, part, sub = np.meshgrid(np.arange(PEERS), np.arange(2), np.arange(width), indexing="ij")
        return (part * N + peer * width + sub).reshape(-1)

    half_forward = forward.copy()
    half_forward[0] = np.concatenate([ones, -sign])
    half_forward[N] = np.concatenate([sign, ones])
    half_inverse = 2.0 * forward.T
    half_inverse[:, 0] = np.concatenate([ones, -sign])
    half_inverse[:, N] = np.concatenate([sign, ones])
    pad = np.zeros((2 * N, 2 * N))
    half_fwd, half_inv = pad.copy(), pad.copy()
    half_fwd[:N] = half_forward[order(2)]
    half_inv[:, :N] = half_inverse[:, order(2)]
    y_fwd = forward[order(4)]
    tables = []
    for stage in (forward, forward.T, y_fwd, y_fwd.T, half_fwd, half_inv):
        high = stage.astype(ml_dtypes.bfloat16)
        tables += [high, (stage - high.astype(np.float64)).astype(ml_dtypes.bfloat16)]
    return np.stack(tables)


def halves(value):
    high = value.astype(BF16)
    return high, (value - high.astype(F32)).astype(BF16)


def mm(a, b):
    return jnp.dot(a, b, preferred_element_type=F32)


def wide(values):
    return jnp.concatenate(values, axis=1)


def tall(values):
    return jnp.concatenate(values, axis=0)


def kernel(own, tables, out, wt, vis, kern, part, inner, plus, minus, take, half_out, half_in, send_f, recv_f, send_b, recv_b,
           table_sem, gather_send, vis_recv, relay_send, f_send, f_recv, f_local, b_send, b_recv, b_local, sum_send, inner_recv,
           plus_recv, minus_recv, give_send, give_recv):
    band, slab = lax.axis_index("band"), lax.axis_index("slab")
    core, column = lax.rem(slab, 2), lax.div(slab, 2)
    z, x_hi = lax.rem(column, 8), lax.div(column, 8)
    y, x = lax.div(band, 2), x_hi * 2 + lax.rem(band, 2)
    home, slot, half = lax.div(band, 4), lax.rem(band, 4), lax.div(z, 4)
    me = (x_hi * 8 + band) * 2 + core
    lower = core == 0
    at = lambda b, s: {"band": b, "slab": s}

    def layer(step, to_core):
        return at(band, (x_hi * 8 + lax.rem(z + step + 8, 8)) * 2 + to_core)

    load = pltpu.make_async_copy(tables, wt, table_sem)
    load.start()

    barrier = pltpu.get_barrier_semaphore()

    def greet_layer(k, _):
        j = lax.rem(me + k, PEERS)
        b, c = lax.rem(lax.div(j, 2), 8), lax.rem(j, 2)
        pl.semaphore_signal(barrier, inc=1, device_id=at(b, (lax.div(j, 16) * 8 + z) * 2 + c), device_id_type=MESH)
        return 0

    def greet_pillar(k, _):
        pl.semaphore_signal(barrier, inc=1, device_id=layer(lax.div(k, 2), lax.rem(k, 2)), device_id_type=MESH)
        return 0

    lax.fori_loop(1, PEERS, greet_layer, 0)
    lax.fori_loop(2, 16, greet_pillar, 0)
    pl.semaphore_wait(barrier, PEERS - 1 + 14)

    turned = [lax.rem(slot + i, 4) for i in range(4)]
    rank = lax.rem(band - z + 8, 8)
    in_held = sum(jnp.where(rank == e, 1, 0) for e in HELD)
    collector = 1 - in_held
    stays = jnp.logical_and(home == core, collector == core)

    def gather(i):
        return pltpu.make_async_remote_copy(
            own.at[pl.ds(turned[i] * N, N)], vis.at[0, rank], gather_send.at[i], vis_recv.at[0, rank],
            device_id=at(4 * core + turned[i], column * 2 + collector), device_id_type=MESH)

    for i in range(1, 4):
        gather(i).start()
    keep = pltpu.make_async_copy(own.at[pl.ds(slot * N, N)], vis.at[0, rank], vis_recv.at[0, rank])
    pl.when(stays)(lambda: keep.start())
    pl.when(jnp.logical_not(stays))(lambda: gather(0).start())

    fold = lambda v: jnp.where(v < N // 2, v, v - N).astype(F32)
    line = lambda dim: lax.broadcasted_iota(jnp.int32, (N, N), dim)
    plane_sq = fold(line(0)) ** 2 + fold(line(1)) ** 2
    scale = N**1.5 / 4.0 / float(N) ** 3

    def coulomb(row):
        ky = fold(jnp.zeros((N, N), jnp.int32) + row)
        squared = plane_sq + ky * ky
        return jnp.where(squared > 0, scale / jnp.maximum(squared, 1.0), 0.0)

    for j in range(4):
        kern[j] = coulomb((x_hi * 8 + band) * 8 + core * 4 + j)
    row = 2 * me + half
    special = jnp.zeros((N, N), jnp.int32) + row == 0
    plain, nyquist = coulomb(row), coulomb(N // 2)
    kern[4] = jnp.where(special, 0.5 * (plain + nyquist), plain)
    kern[5] = jnp.where(special, 0.5 * (plain - nyquist), 0.0)
    flipped = jnp.where(lax.rem(line(0) + line(1), N) == 0, 1.0, 0.0).astype(BF16)
    half_in[...] = jnp.zeros(half_in.shape, F32)

    def left(stage, value, rows=2 * N, depth=2 * N):
        hi, lo = halves(value)
        high, low = wt[2 * stage, :rows, :depth], wt[2 * stage + 1, :rows, :depth]
        return mm(high, hi) + mm(high, lo) + mm(low, hi)

    def right(value, stage):
        hi, lo = halves(value)
        return mm(hi, wt[2 * stage]) + mm(lo, wt[2 * stage]) + mm(hi, wt[2 * stage + 1])

    def distance(k, of_core):
        return k + of_core * (7 - 2 * k)

    def plane_index(of_x_hi, of_band, k, of_core):
        return of_x_hi * 64 + lax.rem(z - distance(k, of_core) + 8, 8) * 8 + of_band

    def chips(visit):
        def step(k, _):
            to_x, to_y = lax.rem(x + lax.rem(k, 4), 4), lax.rem(y + lax.div(k, 4), 4)
            visit(lax.div(to_x, 2), to_y * 2 + lax.rem(to_x, 2))
            return 0
        lax.fori_loop(1, 16, step, 0)

    used = pl.ds(0, USED)

    def send_plane(k):
        mine = plane_index(x_hi, band, k, core)

        def visit(to_x_hi, to_band, to_core):
            pltpu.make_async_remote_copy(
                send_f.at[k, (to_x_hi * 8 + to_band) * 2 + to_core, used], recv_f.at[mine, used], f_send, f_recv,
                device_id=at(to_band, (to_x_hi * 8 + z) * 2 + to_core), device_id_type=MESH).start()

        chips(lambda *chip: [visit(*chip, to_core) for to_core in range(2)])
        visit(x_hi, band, 1 - core)
        pltpu.make_async_copy(send_f.at[k, me, used], recv_f.at[mine, used], f_local.at[k]).start()

    def return_planes(*planes):
        def visit(to_x_hi, to_band):
            for to_core, k in planes:
                pltpu.make_async_remote_copy(
                    send_b.at[plane_index(to_x_hi, to_band, k, to_core), used], recv_b.at[k, me, used], b_send, b_recv.at[k],
                    device_id=at(to_band, (to_x_hi * 8 + z) * 2 + to_core), device_id_type=MESH).start()

        chips(visit)
        for to_core, k in planes:
            @pl.when(core == to_core)
            def _():
                pltpu.make_async_copy(send_b.at[plane_index(x_hi, band, k, to_core), used], recv_b.at[k, me, used],
                                      b_local.at[k]).start()

            @pl.when(core != to_core)
            def _():
                pltpu.make_async_remote_copy(
                    send_b.at[plane_index(x_hi, band, k, to_core), used], recv_b.at[k, me, used], b_send, b_recv.at[k],
                    device_id=at(band, column * 2 + to_core), device_id_type=MESH).start()

    def arrived(k, e):
        pltpu.make_async_copy(vis.at[k, e], vis.at[k, e], vis_recv.at[k, e]).wait()

    def pass_on(here, k, r):
        for end in starts_at(here, r):
            to_core, to_k = place(end, r)
            source, target = (r - here) % 8, (r - end) % 8
            pltpu.make_async_remote_copy(
                vis.at[k, source], vis.at[to_k, target], relay_send, vis_recv.at[to_k, target],
                device_id=layer(stride_of(here, end), to_core), device_id_type=MESH).start()

    def start_plane(of_core, k):
        if k == 0:
            for r in (0, 4, 3, 1) if of_core == 0 else (7, 5, 2, 6):
                arrived(0, r)
                pass_on(0, 0, r)
        here = distance(k, of_core)
        ranks = [(here + e) % 8 for e in HELD]
        if here:
            for r in sorted(ranks, key=lambda r: -len(starts_at(here, r))):
                arrived(k, (r - here) % 8)
                pass_on(here, k, r)

    def analyse(k):
        f0, f1, f3, f4 = [vis[k, e] for e in HELD]
        fields = [f0 * f0, f0 * f1, f1 * f3, f0 * f3, f0 * f4, jnp.zeros((N, N), F32)]
        spec = right(tall([wide(fields[2 * p:2 * p + 2]) for p in range(3)]), INV)
        stacked = [tall([spec[p * N:(p + 1) * N, :N], spec[p * N:(p + 1) * N, N:]]) for p in range(3)]
        full = left(Y_FWD, wide(stacked[:2]))
        for p in range(2):
            send_f[k, :, 8 * p:8 * p + 8, :] = full[:, p * N:(p + 1) * N].reshape(PEERS, 8, N)
        half_out[...] = left(HALF_FWD, stacked[2], rows=N)
        flat = send_f.reshape(4 * PEERS * PITCH, N)
        for i in range(2):
            flat[pl.ds(k * PEERS * PITCH + 16 + i, PEERS, stride=PITCH), :] = half_out[pl.ds(2 * i + half, PEERS, stride=4), :]

    for k in range(4):
        pl.when(lower)(lambda k=k: start_plane(0, k))
        pl.when(jnp.logical_not(lower))(lambda k=k: start_plane(1, k))
        if k == 0:
            load.wait()
        analyse(k)
        send_plane(k)

    flat_f, flat_b = recv_f.reshape(N * PITCH, N), send_b.reshape(N * PITCH, N)
    for k in range(4):
        mine = plane_index(x_hi, band, k, core)
        pltpu.make_async_copy(send_f.at[k, me, used], recv_f.at[mine, used], f_local.at[k]).wait()
    arrivals = recv_f.at[pl.ds(0, 4 * (PEERS - 1)), used]
    pltpu.make_async_copy(arrivals, arrivals, f_recv).wait()

    def strip(r):
        return flat_f[pl.ds(r, N, stride=PITCH), :]

    def store(r, value):
        flat_b[pl.ds(r, N, stride=PITCH), :] = value

    for p in range(2):
        spec = left(FWD, wide([tall([strip(8 * p + j), strip(8 * p + 4 + j)]) for j in range(4)]))
        table = wide([kern[j] for j in range(4)])
        field = left(INV, tall([spec[:N] * table, spec[N:] * table]))
        for j in range(4):
            store(8 * p + j, field[:N, j * N:(j + 1) * N])
            store(8 * p + 4 + j, field[N:, j * N:(j + 1) * N])
    real, imag = strip(16), strip(17)
    hi, lo = halves(tall([real, -imag]))
    spec = left(FWD, wide([tall([real, imag]), mm(hi, flipped) + mm(lo, flipped)]))
    field = left(INV, tall([spec[i * N:(i + 1) * N, :N] * kern[4] + spec[i * N:(i + 1) * N, N:] * kern[5] for i in range(2)]))
    store(16, field[:N])
    store(17, field[N:])
    return_planes((1, 3))
    for k in (3, 2, 1):
        return_planes((0, k), (1, k - 1))
    return_planes((0, 0))

    def synthesise(k):
        mine = plane_index(x_hi, band, k, core)
        pltpu.make_async_copy(send_b.at[mine, used], recv_b.at[k, me, used], b_local.at[k]).wait()
        block = recv_b.at[k, pl.ds(0, PEERS - 1), used]
        pltpu.make_async_copy(block, block, b_recv.at[k]).wait()
        full = left(Y_INV, wide([recv_b[k, :, 8 * p:8 * p + 8, :].reshape(2 * N, N) for p in range(2)]))
        flat = recv_b.reshape(4 * PEERS * PITCH, N)
        for i in range(2):
            half_in[pl.ds(2 * i + half, PEERS, stride=4), :] = flat[pl.ds(k * PEERS * PITCH + 16 + i, PEERS, stride=PITCH), :]
        spec = [full[:, :N], full[:, N:], left(HALF_INV, half_in[...], depth=N)]
        both = right(tall([wide([s[:N], s[N:]]) for s in spec]), FWD)
        fields = [both[(e // 2) * N:(e // 2 + 1) * N, (e % 2) * N:(e % 2 + 1) * N] for e in range(5)]
        f0, f1, f3, f4 = [vis[k, e] for e in HELD]
        part[k, 0] = fields[0] * f0 + fields[1] * f1 + fields[3] * f3 + fields[4] * f4
        part[k, 1] = fields[1] * f0 + fields[2] * f3
        part[k, 3] = fields[2] * f1 + fields[3] * f0
        part[k, 4] = fields[4] * f0

    def pass_sums(of_core, k):
        here = distance(k, of_core)
        ranks = [(here + e) % 8 for e in HELD]
        for r in sorted(ranks, key=lambda r: len(starts_at(here, r))):
            e = (r - here) % 8
            if starts_at(here, r):
                pltpu.make_async_copy(inner.at[k, e], inner.at[k, e], inner_recv.at[k, e]).wait()
                part[k, e] += inner[k, e]
            (back,) = [start for start, end in ROUTES[r] if end == here]
            step = stride_of(back, here)
            to_core, to_k = place(back, r)
            to_e = (r - back) % 8
            target, sem = (inner, inner_recv) if back else (plus, plus_recv) if step > 0 else (minus, minus_recv)
            index = (to_k, to_e) if back else (r,)
            pltpu.make_async_remote_copy(part.at[k, e], target.at[index], sum_send, sem.at[index],
                                         device_id=layer(-step, to_core), device_id_type=MESH).start()

    for k in (3, 2, 1, 0):
        synthesise(k)
        if k:
            pl.when(lower)(lambda k=k: pass_sums(0, k))
        pl.when(jnp.logical_not(lower))(lambda k=k: pass_sums(1, k))

    mine = take.at[pl.ds(slot * N, N)]

    def give(r):
        return pltpu.make_async_remote_copy(part.at[0, r], mine, give_send.at[r], give_recv.at[slot],
                                            device_id=at(lax.rem(z + r, 8), column * 2 + home), device_id_type=MESH)

    def keeps(r):
        return jnp.logical_and(home == core, rank == r)

    def finish(ranks):
        for r in ranks:
            total = part[0, r] if r in HELD else None
            strides = [stride_of(0, end) for end in starts_at(0, r)]
            for ref, sem, sign in ((plus, plus_recv, 1), (minus, minus_recv, -1)):
                if any(step * sign > 0 for step in strides):
                    pltpu.make_async_copy(ref.at[r], ref.at[r], sem.at[r]).wait()
                    total = ref[r] if total is None else total + ref[r]
            part[0, r] = -0.25 * total
            pl.when(keeps(r))(lambda r=r: pltpu.make_async_copy(part.at[0, r], mine, give_recv.at[slot]).start())
            pl.when(jnp.logical_not(keeps(r)))(lambda r=r: give(r).start())

    pl.when(lower)(lambda: finish((4, 1, 0, 3)))
    pl.when(jnp.logical_not(lower))(lambda: finish((5, 6, 7, 2)))

    for q in range(4):
        block = take.at[pl.ds(q * N, N)]
        pltpu.make_async_copy(block, block, give_recv.at[q]).wait()
    out[...] = take[...]

    for i in range(1, 4):
        gather(i).wait_send()
    pl.when(jnp.logical_not(stays))(lambda: gather(0).wait_send())
    for sem, source in ((f_send, recv_f), (b_send, send_b)):
        block = source.at[pl.ds(0, 4 * (PEERS - 1)), used]
        pltpu.make_async_copy(block, block, sem).wait()

    def left_by(sem, ref, count):
        block = ref.reshape(32 * N, N).at[pl.ds(0, count * N)]
        pltpu.make_async_copy(block, block, sem).wait()

    def settle(ranks, relays, sums):
        left_by(relay_send, vis, relays)
        left_by(sum_send, part, sums)
        for r in ranks:
            pl.when(jnp.logical_not(keeps(r)))(lambda r=r: give(r).wait_send())

    pl.when(lower)(lambda: settle((0, 1, 3, 4), 13, 12))
    pl.when(jnp.logical_not(lower))(lambda: settle((2, 5, 6, 7), 15, 16))


def per_device(wavefunctions, tables):
    dma = pltpu.SemaphoreType.DMA
    planes = lambda *shape: pltpu.VMEM((*shape, N, N), F32)
    by_peer, by_plane = pltpu.VMEM((4, PEERS, PITCH, N), F32), pltpu.VMEM((N, PITCH, N), F32)
    field = pl.pallas_call(
        kernel,
        out_shape=jax.ShapeDtypeStruct((4 * N, N), F32),
        in_specs=[pl.BlockSpec(memory_space=pltpu.HBM)] * 2,
        out_specs=pl.BlockSpec(memory_space=pltpu.VMEM),
        scratch_shapes=[
            pltpu.VMEM(tables.shape, BF16), planes(4, 8), planes(6), planes(4, 8), planes(4, 8), planes(8), planes(8),
            pltpu.VMEM((4 * N, N), F32), planes(), planes(), by_peer, by_plane, by_plane, by_peer,
            dma, dma((4,)), dma((4, 8)), dma, dma, dma, dma((4,)), dma, dma((4,)), dma((4,)), dma, dma((4, 8)),
            dma((8,)), dma((8,)), dma((8,)), dma((4,)),
        ],
        compiler_params=pltpu.CompilerParams(collective_id=0, has_side_effects=True, vmem_limit_bytes=48 << 20),
        name="exchange",
    )(*[pltpu.with_memory_space_constraint(value, pltpu.HBM) for value in (wavefunctions.reshape(4 * N, N), tables)])
    return field.reshape(1, 4, N, N)


def solution(mesh):
    tables = weight_tables()
    spec = P("band", "slab", None, None)
    run = jax.shard_map(per_device, mesh=mesh, in_specs=(spec, P()), out_specs=spec, check_vma=False)
    return lambda wavefunctions: run(wavefunctions, jnp.asarray(tables))
```

profile of v0, /device:TPU:1, one launch (start us, length us, event | category | flops | bytes accessed | tf_op | source)
XLA Modules:
  0.0 74.1 jit_solution(15464232230646914146)
XLA Ops:
  0.0 73.4 %exchange.1 = f32[512,128]{1,0:T(8,128)S(1)} custom-call(f32[512,128]{1,0:T(8,128)} %bitcast.3, bf16[12,256,256]{2,1,0:T(8,128)(2,1)} %constant.2.clone.tables), custom_call_target="tpu_custom_call" | custom-call | tf_op jit(solution)/shard_map/exchange/pallas_call | solution.py:392
  73.4 0.7 copy.4
where the time goes:
time: 74.2 us; the launch traced here: 74.1 us
  Pallas kernels  73.4 us (99%)
    pallas_call x1, Pallas kernels, per_device(): pl.pallas_call(kernel, out_shape=jax.ShapeDtypeStruct((4 * N, N), F32), i...  73.4 us

commit v1 on v0

--- a/solution.py
+++ b/solution.py
@@ -43,6 +43,11 @@
 
 def starts_at(distance, r):
     return [end for start, end in ROUTES[r] if start == distance]
+
+
+def sides(r):
+    strides = [stride_of(0, end) for end in starts_at(0, r)]
+    return [side for side, present in enumerate((max(strides) > 0, min(strides) < 0, r in HELD)) if present]
 
 
 def weight_tables():
@@ -92,9 +97,9 @@
     return jnp.concatenate(values, axis=0)
 
 
-def kernel(own, tables, out, wt, vis, kern, part, inner, plus, minus, take, half_out, half_in, send_f, recv_f, send_b, recv_b,
+def kernel(own, tables, out, wt, vis, kern, part, inner, arrive, half_out, half_in, send_f, recv_f, send_b, recv_b,
            table_sem, gather_send, vis_recv, relay_send, f_send, f_recv, f_local, b_send, b_recv, b_local, sum_send, inner_recv,
-           plus_recv, minus_recv, give_send, give_recv):
+           arrive_recv):
     band, slab = lax.axis_index("band"), lax.axis_index("slab")
     core, column = lax.rem(slab, 2), lax.div(slab, 2)
     z, x_hi = lax.rem(column, 8), lax.div(column, 8)
@@ -131,6 +136,10 @@
     in_held = sum(jnp.where(rank == e, 1, 0) for e in HELD)
     collector = 1 - in_held
     stays = jnp.logical_and(home == core, collector == core)
+
+    def by_rank(visit):
+        for r in range(8):
+            pl.when(rank == r)(lambda r=r: visit(r))
 
     def gather(i):
         return pltpu.make_async_remote_copy(
@@ -179,11 +188,16 @@
         return of_x_hi * 64 + lax.rem(z - distance(k, of_core) + 8, 8) * 8 + of_band
 
     def chips(visit):
+        tos = [(lax.div(t, 2), lax.rem(t, 2)) for t in (lax.rem(x + i, 4) for i in (2, 1, 3, 0))]
+
         def step(k, _):
-            to_x, to_y = lax.rem(x + lax.rem(k, 4), 4), lax.rem(y + lax.div(k, 4), 4)
-            visit(lax.div(to_x, 2), to_y * 2 + lax.rem(to_x, 2))
+            to_y = lax.rem(y + lax.rem(k * 2, 4) + lax.div(k, 2), 4) * 2
+            for to_hi, to_lo in tos:
+                visit(to_hi, to_y + to_lo)
             return 0
-        lax.fori_loop(1, 16, step, 0)
+        lax.fori_loop(1, 4, step, 0)
+        for to_hi, to_lo in tos[:3]:
+            visit(to_hi, y * 2 + to_lo)
 
     used = pl.ds(0, USED)
 
@@ -322,12 +336,19 @@
                 part[k, e] += inner[k, e]
             (back,) = [start for start, end in ROUTES[r] if end == here]
             step = stride_of(back, here)
-            to_core, to_k = place(back, r)
-            to_e = (r - back) % 8
-            target, sem = (inner, inner_recv) if back else (plus, plus_recv) if step > 0 else (minus, minus_recv)
-            index = (to_k, to_e) if back else (r,)
-            pltpu.make_async_remote_copy(part.at[k, e], target.at[index], sum_send, sem.at[index],
-                                         device_id=layer(-step, to_core), device_id_type=MESH).start()
+            if back:
+                to_core, to_k = place(back, r)
+                index = (to_k, (r - back) % 8)
+                pltpu.make_async_remote_copy(part.at[k, e], inner.at[index], sum_send, inner_recv.at[index],
+                                             device_id=layer(-step, to_core), device_id_type=MESH).start()
+            else:
+                hand_in(k, e, r, -step, 0 if step > 0 else 1).start()
+
+    def hand_in(k, e, r, step, side):
+        to_z = lax.rem(z + step + 8, 8)
+        return pltpu.make_async_remote_copy(
+            part.at[k, e], arrive.at[side, slot], sum_send, arrive_recv.at[side, slot],
+            device_id=at(lax.rem(to_z + r, 8), (x_hi * 8 + to_z) * 2 + home), device_id_type=MESH)
 
     for k in (3, 2, 1, 0):
         synthesise(k)
@@ -335,34 +356,21 @@
             pl.when(lower)(lambda k=k: pass_sums(0, k))
         pl.when(jnp.logical_not(lower))(lambda k=k: pass_sums(1, k))
 
-    mine = take.at[pl.ds(slot * N, N)]
-
-    def give(r):
-        return pltpu.make_async_remote_copy(part.at[0, r], mine, give_send.at[r], give_recv.at[slot],
-                                            device_id=at(lax.rem(z + r, 8), column * 2 + home), device_id_type=MESH)
-
-    def keeps(r):
-        return jnp.logical_and(home == core, rank == r)
-
-    def finish(ranks):
-        for r in ranks:
-            total = part[0, r] if r in HELD else None
-            strides = [stride_of(0, end) for end in starts_at(0, r)]
-            for ref, sem, sign in ((plus, plus_recv, 1), (minus, minus_recv, -1)):
-                if any(step * sign > 0 for step in strides):
-                    pltpu.make_async_copy(ref.at[r], ref.at[r], sem.at[r]).wait()
-                    total = ref[r] if total is None else total + ref[r]
-            part[0, r] = -0.25 * total
-            pl.when(keeps(r))(lambda r=r: pltpu.make_async_copy(part.at[0, r], mine, give_recv.at[slot]).start())
-            pl.when(jnp.logical_not(keeps(r)))(lambda r=r: give(r).start())
-
-    pl.when(lower)(lambda: finish((4, 1, 0, 3)))
-    pl.when(jnp.logical_not(lower))(lambda: finish((5, 6, 7, 2)))
-
-    for q in range(4):
-        block = take.at[pl.ds(q * N, N)]
-        pltpu.make_async_copy(block, block, give_recv.at[q]).wait()
-    out[...] = take[...]
+    @pl.when(lower)
+    def _():
+        for r in HELD:
+            keeps = jnp.logical_and(home == 0, rank == r)
+            local = pltpu.make_async_copy(part.at[0, r], arrive.at[2, slot], arrive_recv.at[2, slot])
+            pl.when(keeps)(lambda: local.start())
+            pl.when(jnp.logical_not(keeps))(lambda: hand_in(0, r, r, 0, 2).start())
+
+    def total_up(r):
+        for q in range(4):
+            for side in sides(r):
+                pltpu.make_async_copy(arrive.at[side, q], arrive.at[side, q], arrive_recv.at[side, q]).wait()
+            out[q * N:(q + 1) * N] = -0.25 * sum(arrive[side, q] for side in sides(r))
+
+    by_rank(total_up)
 
     for i in range(1, 4):
         gather(i).wait_send()
@@ -375,14 +383,11 @@
         block = ref.reshape(32 * N, N).at[pl.ds(0, count * N)]
         pltpu.make_async_copy(block, block, sem).wait()
 
-    def settle(ranks, relays, sums):
-        left_by(relay_send, vis, relays)
-        left_by(sum_send, part, sums)
-        for r in ranks:
-            pl.when(jnp.logical_not(keeps(r)))(lambda r=r: give(r).wait_send())
-
-    pl.when(lower)(lambda: settle((0, 1, 3, 4), 13, 12))
-    pl.when(jnp.logical_not(lower))(lambda: settle((2, 5, 6, 7), 15, 16))
+    pl.when(lower)(lambda: left_by(relay_send, vis, 13))
+    pl.when(jnp.logical_not(lower))(lambda: left_by(relay_send, vis, 15))
+    kept = jnp.logical_and(jnp.logical_and(lower, home == 0), in_held == 1)
+    pl.when(kept)(lambda: left_by(sum_send, part, 15))
+    pl.when(jnp.logical_not(kept))(lambda: left_by(sum_send, part, 16))
 
 
 def per_device(wavefunctions, tables):
@@ -395,10 +400,8 @@
         in_specs=[pl.BlockSpec(memory_space=pltpu.HBM)] * 2,
         out_specs=pl.BlockSpec(memory_space=pltpu.VMEM),
         scratch_shapes=[
-            pltpu.VMEM(tables.shape, BF16), planes(4, 8), planes(6), planes(4, 8), planes(4, 8), planes(8), planes(8),
-            pltpu.VMEM((4 * N, N), F32), planes(), planes(), by_peer, by_plane, by_plane, by_peer,
-            dma, dma((4,)), dma((4, 8)), dma, dma, dma, dma((4,)), dma, dma((4,)), dma((4,)), dma, dma((4, 8)),
-            dma((8,)), dma((8,)), dma((8,)), dma((4,)),
+            pltpu.VMEM(tables.shape, BF16), planes(4, 8), planes(6), planes(4, 8), planes(4, 8), planes(3, 4), planes(), planes(), by_peer, by_plane, by_plane, by_peer,
+            dma, dma((4,)), dma((4, 8)), dma, dma, dma, dma((4,)), dma, dma((4,)), dma((4,)), dma, dma((4, 8)), dma((3, 4)),
         ],
         compiler_params=pltpu.CompilerParams(collective_id=0, has_side_effects=True, vmem_limit_bytes=48 << 20),
         name="exchange",

time: 74.2 us -> 71.2 us (0.960)
  Pallas kernels: 73.4 us -> 70.4 us
    pallas_call x1, Pallas kernels: 73.4 us -> 70.4 us  [per_device(): pl.pallas_call(kernel, out_shape=jax.ShapeDtypeStruct((4 * N, N), F32), i...]
where the time goes in v1:
time: 71.2 us; the launch traced here: 71.1 us
  Pallas kernels  70.4 us (99%)
    pallas_call x1, Pallas kernels, per_device(): pl.pallas_call(kernel, out_shape=jax.ShapeDtypeStruct((4 * N, N), F32), i...  70.4 us

profile of v1, /device:TPU:1, one launch (start us, length us, event | category | flops | bytes accessed | tf_op | source)
XLA Modules:
  0.0 71.1 jit_solution(2387651458727448109)
XLA Ops:
  0.0 70.4 %exchange.1 = f32[512,128]{1,0:T(8,128)S(1)} custom-call(f32[512,128]{1,0:T(8,128)} %bitcast.3, bf16[12,256,256]{2,1,0:T(8,128)(2,1)} %constant.2.clone.tables), custom_call_target="tpu_custom_call" | custom-call | tf_op jit(solution)/shard_map/exchange/pallas_call | solution.py:397
  70.4 0.7 copy.4

commit v2 on v1

--- a/solution.py
+++ b/solution.py
@@ -12,6 +12,7 @@
 PEERS = 32
 USED, PITCH = 18, 24
 BF16, F32 = jnp.bfloat16, jnp.float32
+ALL, FIRST, REST = (0, USED), (0, 8), (8, USED - 8)
 FWD, INV, Y_FWD, Y_INV, HALF_FWD, HALF_INV = range(6)
 
 HELD = (0, 1, 3, 4)
@@ -99,7 +100,7 @@
 
 def kernel(own, tables, out, wt, vis, kern, part, inner, arrive, half_out, half_in, send_f, recv_f, send_b, recv_b,
            table_sem, gather_send, vis_recv, relay_send, f_send, f_recv, f_local, b_send, b_recv, b_local, sum_send, inner_recv,
-           arrive_recv):
+           arrive_recv, ready):
     band, slab = lax.axis_index("band"), lax.axis_index("slab")
     core, column = lax.rem(slab, 2), lax.div(slab, 2)
     z, x_hi = lax.rem(column, 8), lax.div(column, 8)
@@ -117,19 +118,21 @@
 
     barrier = pltpu.get_barrier_semaphore()
 
-    def greet_layer(k, _):
-        j = lax.rem(me + k, PEERS)
-        b, c = lax.rem(lax.div(j, 2), 8), lax.rem(j, 2)
-        pl.semaphore_signal(barrier, inc=1, device_id=at(b, (lax.div(j, 16) * 8 + z) * 2 + c), device_id_type=MESH)
-        return 0
+    def greet_group(semaphore):
+        def greet(k, _):
+            j = lax.rem(band * 2 + core + k, 16)
+            pl.semaphore_signal(semaphore, inc=1, device_id=at(lax.div(j, 2), column * 2 + lax.rem(j, 2)), device_id_type=MESH)
+            return 0
+        lax.fori_loop(1, 16, greet, 0)
 
     def greet_pillar(k, _):
         pl.semaphore_signal(barrier, inc=1, device_id=layer(lax.div(k, 2), lax.rem(k, 2)), device_id_type=MESH)
         return 0
 
-    lax.fori_loop(1, PEERS, greet_layer, 0)
+    greet_group(barrier)
     lax.fori_loop(2, 16, greet_pillar, 0)
-    pl.semaphore_wait(barrier, PEERS - 1 + 14)
+    pl.semaphore_signal(barrier, inc=1, device_id=at(band, ((1 - x_hi) * 8 + z) * 2 + core), device_id_type=MESH)
+    pl.semaphore_wait(barrier, 15 + 14 + 1)
 
     turned = [lax.rem(slot + i, 4) for i in range(4)]
     rank = lax.rem(band - z + 8, 8)
@@ -151,6 +154,8 @@
     keep = pltpu.make_async_copy(own.at[pl.ds(slot * N, N)], vis.at[0, rank], vis_recv.at[0, rank])
     pl.when(stays)(lambda: keep.start())
     pl.when(jnp.logical_not(stays))(lambda: gather(0).start())
+
+    greet_group(ready)
 
     fold = lambda v: jnp.where(v < N // 2, v, v - N).astype(F32)
     line = lambda dim: lax.broadcasted_iota(jnp.int32, (N, N), dim)
@@ -201,43 +206,48 @@
 
     used = pl.ds(0, USED)
 
-    def send_plane(k):
+    def own_rows(k, rows, sem):
+        mine, rows = plane_index(x_hi, band, k, core), pl.ds(*rows)
+        return pltpu.make_async_copy(send_f.at[k, me, rows], recv_f.at[mine, rows], f_local.at[k + sem // 2])
+
+    def send_plane(k, rows, sem):
         mine = plane_index(x_hi, band, k, core)
 
         def visit(to_x_hi, to_band, to_core):
             pltpu.make_async_remote_copy(
-                send_f.at[k, (to_x_hi * 8 + to_band) * 2 + to_core, used], recv_f.at[mine, used], f_send, f_recv,
+                send_f.at[k, (to_x_hi * 8 + to_band) * 2 + to_core, pl.ds(*rows)], recv_f.at[mine, pl.ds(*rows)], f_send,
+                f_recv.at[sem],
                 device_id=at(to_band, (to_x_hi * 8 + z) * 2 + to_core), device_id_type=MESH).start()
 
         chips(lambda *chip: [visit(*chip, to_core) for to_core in range(2)])
         visit(x_hi, band, 1 - core)
-        pltpu.make_async_copy(send_f.at[k, me, used], recv_f.at[mine, used], f_local.at[k]).start()
-
-    def return_planes(*planes):
+        own_rows(k, rows, sem).start()
+
+    def return_planes(*planes, rows=ALL):
         def visit(to_x_hi, to_band):
             for to_core, k in planes:
                 pltpu.make_async_remote_copy(
-                    send_b.at[plane_index(to_x_hi, to_band, k, to_core), used], recv_b.at[k, me, used], b_send, b_recv.at[k],
+                    send_b.at[plane_index(to_x_hi, to_band, k, to_core), pl.ds(*rows)], recv_b.at[k, me, pl.ds(*rows)], b_send, b_recv.at[k],
                     device_id=at(to_band, (to_x_hi * 8 + z) * 2 + to_core), device_id_type=MESH).start()
 
         chips(visit)
         for to_core, k in planes:
             @pl.when(core == to_core)
             def _():
-                pltpu.make_async_copy(send_b.at[plane_index(x_hi, band, k, to_core), used], recv_b.at[k, me, used],
-                                      b_local.at[k]).start()
+                pltpu.make_async_copy(send_b.at[plane_index(x_hi, band, k, to_core), pl.ds(*rows)], recv_b.at[k, me, pl.ds(*rows)],
+                                      b_local.at[k + (rows == REST)]).start()
 
             @pl.when(core != to_core)
             def _():
                 pltpu.make_async_remote_copy(
-                    send_b.at[plane_index(x_hi, band, k, to_core), used], recv_b.at[k, me, used], b_send, b_recv.at[k],
+                    send_b.at[plane_index(x_hi, band, k, to_core), pl.ds(*rows)], recv_b.at[k, me, pl.ds(*rows)], b_send, b_recv.at[k],
                     device_id=at(band, column * 2 + to_core), device_id_type=MESH).start()
 
     def arrived(k, e):
         pltpu.make_async_copy(vis.at[k, e], vis.at[k, e], vis_recv.at[k, e]).wait()
 
-    def pass_on(here, k, r):
-        for end in starts_at(here, r):
+    def pass_on(here, k, r, ends=None):
+        for end in starts_at(here, r) if ends is None else ends:
             to_core, to_k = place(end, r)
             source, target = (r - here) % 8, (r - end) % 8
             pltpu.make_async_remote_copy(
@@ -246,9 +256,12 @@
 
     def start_plane(of_core, k):
         if k == 0:
-            for r in (0, 4, 3, 1) if of_core == 0 else (7, 5, 2, 6):
+            mine = (0, 4, 3, 1) if of_core == 0 else (7, 5, 2, 6)
+            for r in mine:
                 arrived(0, r)
-                pass_on(0, 0, r)
+                pass_on(0, 0, r, [end for end in starts_at(0, r) if end in (1, 7)])
+            for r in mine:
+                pass_on(0, 0, r, [end for end in starts_at(0, r) if end not in (1, 7)])
         here = distance(k, of_core)
         ranks = [(here + e) % 8 for e in HELD]
         if here:
@@ -258,13 +271,14 @@
 
     def analyse(k):
         f0, f1, f3, f4 = [vis[k, e] for e in HELD]
-        fields = [f0 * f0, f0 * f1, f1 * f3, f0 * f3, f0 * f4, jnp.zeros((N, N), F32)]
-        spec = right(tall([wide(fields[2 * p:2 * p + 2]) for p in range(3)]), INV)
-        stacked = [tall([spec[p * N:(p + 1) * N, :N], spec[p * N:(p + 1) * N, N:]]) for p in range(3)]
-        full = left(Y_FWD, wide(stacked[:2]))
-        for p in range(2):
-            send_f[k, :, 8 * p:8 * p + 8, :] = full[:, p * N:(p + 1) * N].reshape(PEERS, 8, N)
-        half_out[...] = left(HALF_FWD, stacked[2], rows=N)
+        spec = right(wide([f0 * f0, f0 * f1]), INV)
+        send_f[k, :, 0:8, :] = left(Y_FWD, tall([spec[:, :N], spec[:, N:]])).reshape(PEERS, 8, N)
+        if k == 3:
+            send_plane(k, FIRST, 1)
+        spec = right(tall([wide([f1 * f3, f0 * f3]), wide([f0 * f4, jnp.zeros((N, N), F32)])]), INV)
+        stacked = [tall([spec[p * N:(p + 1) * N, :N], spec[p * N:(p + 1) * N, N:]]) for p in range(2)]
+        send_f[k, :, 8:16, :] = left(Y_FWD, stacked[0]).reshape(PEERS, 8, N)
+        half_out[...] = left(HALF_FWD, stacked[1], rows=N)
         flat = send_f.reshape(4 * PEERS * PITCH, N)
         for i in range(2):
             flat[pl.ds(k * PEERS * PITCH + 16 + i, PEERS, stride=PITCH), :] = half_out[pl.ds(2 * i + half, PEERS, stride=4), :]
@@ -274,15 +288,20 @@
         pl.when(jnp.logical_not(lower))(lambda k=k: start_plane(1, k))
         if k == 0:
             load.wait()
+            pl.semaphore_wait(ready, 15)
         analyse(k)
-        send_plane(k)
+        send_plane(k, REST if k == 3 else ALL, 2 if k == 3 else 0)
 
     flat_f, flat_b = recv_f.reshape(N * PITCH, N), send_b.reshape(N * PITCH, N)
-    for k in range(4):
-        mine = plane_index(x_hi, band, k, core)
-        pltpu.make_async_copy(send_f.at[k, me, used], recv_f.at[mine, used], f_local.at[k]).wait()
-    arrivals = recv_f.at[pl.ds(0, 4 * (PEERS - 1)), used]
-    pltpu.make_async_copy(arrivals, arrivals, f_recv).wait()
+    def received(sem, planes, rows):
+        block = recv_f.at[pl.ds(0, planes * (PEERS - 1)), pl.ds(*rows)]
+        pltpu.make_async_copy(block, block, f_recv.at[sem]).wait()
+
+    for k in range(3):
+        own_rows(k, ALL, 0).wait()
+    received(0, 3, ALL)
+    own_rows(3, FIRST, 1).wait()
+    received(1, 1, FIRST)
 
     def strip(r):
         return flat_f[pl.ds(r, N, stride=PITCH), :]
@@ -291,26 +310,45 @@
         flat_b[pl.ds(r, N, stride=PITCH), :] = value
 
     for p in range(2):
+        if p == 1:
+            own_rows(3, REST, 2).wait()
+            received(2, 1, REST)
         spec = left(FWD, wide([tall([strip(8 * p + j), strip(8 * p + 4 + j)]) for j in range(4)]))
         table = wide([kern[j] for j in range(4)])
         field = left(INV, tall([spec[:N] * table, spec[N:] * table]))
         for j in range(4):
             store(8 * p + j, field[:N, j * N:(j + 1) * N])
             store(8 * p + 4 + j, field[N:, j * N:(j + 1) * N])
+        if p == 0:
+            return_planes((1, 3), rows=FIRST)
     real, imag = strip(16), strip(17)
     hi, lo = halves(tall([real, -imag]))
     spec = left(FWD, wide([tall([real, imag]), mm(hi, flipped) + mm(lo, flipped)]))
     field = left(INV, tall([spec[i * N:(i + 1) * N, :N] * kern[4] + spec[i * N:(i + 1) * N, N:] * kern[5] for i in range(2)]))
     store(16, field[:N])
     store(17, field[N:])
-    return_planes((1, 3))
+    return_planes((1, 3), rows=REST)
     for k in (3, 2, 1):
         return_planes((0, k), (1, k - 1))
     return_planes((0, 0))
 
     def synthesise(k):
         mine = plane_index(x_hi, band, k, core)
-        pltpu.make_async_copy(send_b.at[mine, used], recv_b.at[k, me, used], b_local.at[k]).wait()
+        def mine_back(rows, sem):
+            rows = pl.ds(*rows)
+            return pltpu.make_async_copy(send_b.at[mine, rows], recv_b.at[k, me, rows], b_local.at[sem])
+
+        if k == 3:
+            @pl.when(lower)
+            def _():
+                mine_back(ALL, 3).wait()
+
+            @pl.when(jnp.logical_not(lower))
+            def _():
+                mine_back(FIRST, 3).wait()
+                mine_back(REST, 4).wait()
+        else:
+            mine_back(ALL, k).wait()
         block = recv_b.at[k, pl.ds(0, PEERS - 1), used]
         pltpu.make_async_copy(block, block, b_recv.at[k]).wait()
         full = left(Y_INV, wide([recv_b[k, :, 8 * p:8 * p + 8, :].reshape(2 * N, N) for p in range(2)]))
@@ -401,7 +439,8 @@
         out_specs=pl.BlockSpec(memory_space=pltpu.VMEM),
         scratch_shapes=[
             pltpu.VMEM(tables.shape, BF16), planes(4, 8), planes(6), planes(4, 8), planes(4, 8), planes(3, 4), planes(), planes(), by_peer, by_plane, by_plane, by_peer,
-            dma, dma((4,)), dma((4, 8)), dma, dma, dma, dma((4,)), dma, dma((4,)), dma((4,)), dma, dma((4, 8)), dma((3, 4)),
+            dma, dma((4,)), dma((4, 8)), dma, dma, dma((3,)), dma((5,)), dma, dma((4,)), dma((5,)), dma, dma((4, 8)), dma((3, 4)),
+            pltpu.SemaphoreType.REGULAR,
         ],
         compiler_params=pltpu.CompilerParams(collective_id=0, has_side_effects=True, vmem_limit_bytes=48 << 20),
         name="exchange",

time: 71.2 us -> 69.6 us (0.978)
  Pallas kernels: 70.4 us -> 68.4 us
    pallas_call x1, Pallas kernels: 70.4 us -> 68.4 us  [per_device(): pl.pallas_call(kernel, out_shape=jax.ShapeDtypeStruct((4 * N, N), F32), i...]
where the time goes in v2:
time: 69.6 us; the launch traced here: 69.1 us
  Pallas kernels  68.4 us (98%)
  local copies, waits for them, and re-layouts  0.71 us (1%)
    pallas_call x1, Pallas kernels, per_device(): pl.pallas_call(kernel, out_shape=jax.ShapeDtypeStruct((4 * N, N), F32), i...  68.4 us

profile of v2, /device:TPU:1, one launch (start us, length us, event | category | flops | bytes accessed | tf_op | source)
XLA Modules:
  0.0 69.1 jit_solution(5095826334542833131)
XLA Ops:
  0.0 68.4 %exchange.1 = f32[512,128]{1,0:T(8,128)S(1)} custom-call(f32[512,128]{1,0:T(8,128)} %bitcast.3, bf16[12,256,256]{2,1,0:T(8,128)(2,1)} %constant.2.clone.tables), custom_call_target="tpu_custom_call" | custom-call | tf_op jit(solution)/shard_map/exchange/pallas_call | solution.py:435
  68.4 0.7 %copy.4 = f32[1,4,128,128]{3,2,1,0:T(8,128)} copy(f32[1,4,128,128]{3,2,1,0:T(8,128)S(1)} %bitcast.2) | data formatting | bytes 524288

commit v3 on v2

--- a/solution.py
+++ b/solution.py
@@ -13,6 +13,7 @@
 USED, PITCH = 18, 24
 BF16, F32 = jnp.bfloat16, jnp.float32
 ALL, FIRST, REST = (0, USED), (0, 8), (8, USED - 8)
+ORDER = [(2, 2), (1, 1), (3, 3), (2, 1), (3, 1), (1, 3), (2, 3), (1, 2), (3, 2), (1, 0), (0, 3), (3, 0), (0, 1), (2, 0), (0, 2)]
 FWD, INV, Y_FWD, Y_INV, HALF_FWD, HALF_INV = range(6)
 
 HELD = (0, 1, 3, 4)
@@ -193,16 +194,11 @@
         return of_x_hi * 64 + lax.rem(z - distance(k, of_core) + 8, 8) * 8 + of_band
 
     def chips(visit):
-        tos = [(lax.div(t, 2), lax.rem(t, 2)) for t in (lax.rem(x + i, 4) for i in (2, 1, 3, 0))]
-
-        def step(k, _):
-            to_y = lax.rem(y + lax.rem(k * 2, 4) + lax.div(k, 2), 4) * 2
-            for to_hi, to_lo in tos:
-                visit(to_hi, to_y + to_lo)
-            return 0
-        lax.fori_loop(1, 4, step, 0)
-        for to_hi, to_lo in tos[:3]:
-            visit(to_hi, y * 2 + to_lo)
+        at_x = [(lax.div(t, 2), lax.rem(t, 2)) for t in (lax.rem(x + i, 4) for i in range(4))]
+        at_y = [lax.rem(y + i, 4) * 2 for i in range(4)]
+        for i, j in ORDER:
+            to_hi, to_lo = at_x[i]
+            visit(to_hi, at_y[j] + to_lo)
 
     used = pl.ds(0, USED)
 
@@ -329,7 +325,8 @@
     store(17, field[N:])
     return_planes((1, 3), rows=REST)
     for k in (3, 2, 1):
-        return_planes((0, k), (1, k - 1))
+        return_planes((0, k))
+        return_planes((1, k - 1))
     return_planes((0, 0))
 
     def synthesise(k):

time: 69.6 us -> 69.4 us (level)
  no operation moved by 1% of the time
where the time goes in v3:
time: 69.4 us; the launch traced here: 69.3 us
  Pallas kernels  68.6 us (99%)
  local copies, waits for them, and re-layouts  0.71 us (1%)
    pallas_call x1, Pallas kernels, per_device(): pl.pallas_call(kernel, out_shape=jax.ShapeDtypeStruct((4 * N, N), F32), i...  68.6 us

profile of v3, /device:TPU:1, one launch (start us, length us, event | category | flops | bytes accessed | tf_op | source)
XLA Modules:
  0.0 69.3 jit_solution(16697141825089886542)
XLA Ops:
  0.0 68.6 %exchange.1 = f32[512,128]{1,0:T(8,128)S(1)} custom-call(f32[512,128]{1,0:T(8,128)} %bitcast.3, bf16[12,256,256]{2,1,0:T(8,128)(2,1)} %constant.2.clone.tables), custom_call_target="tpu_custom_call" | custom-call | tf_op jit(solution)/shard_map/exchange/pallas_call | solution.py:432
  68.6 0.7 %copy.4 = f32[1,4,128,128]{3,2,1,0:T(8,128)} copy(f32[1,4,128,128]{3,2,1,0:T(8,128)S(1)} %bitcast.2) | data formatting | bytes 524288

commit v4 on v3

--- a/solution.py
+++ b/solution.py
@@ -12,6 +12,7 @@
 PEERS = 32
 USED, PITCH = 18, 24
 BF16, F32 = jnp.bfloat16, jnp.float32
+COLLECTED = ((2, 3), (6, 1))
 ALL, FIRST, REST = (0, USED), (0, 8), (8, USED - 8)
 ORDER = [(2, 2), (1, 1), (3, 3), (2, 1), (3, 1), (1, 3), (2, 3), (1, 2), (3, 2), (1, 0), (0, 3), (3, 0), (0, 1), (2, 0), (0, 2)]
 FWD, INV, Y_FWD, Y_INV, HALF_FWD, HALF_INV = range(6)
@@ -48,7 +49,7 @@
 
 
 def sides(r):
-    strides = [stride_of(0, end) for end in starts_at(0, r)]
+    strides = [stride_of(0, end) for end in starts_at(0, r) if (end, r) not in COLLECTED]
     return [side for side, present in enumerate((max(strides) > 0, min(strides) < 0, r in HELD)) if present]
 
 
@@ -316,18 +317,17 @@
             store(8 * p + j, field[:N, j * N:(j + 1) * N])
             store(8 * p + 4 + j, field[N:, j * N:(j + 1) * N])
         if p == 0:
-            return_planes((1, 3), rows=FIRST)
+            return_planes((1, 3), (0, 3), rows=FIRST)
     real, imag = strip(16), strip(17)
     hi, lo = halves(tall([real, -imag]))
     spec = left(FWD, wide([tall([real, imag]), mm(hi, flipped) + mm(lo, flipped)]))
     field = left(INV, tall([spec[i * N:(i + 1) * N, :N] * kern[4] + spec[i * N:(i + 1) * N, N:] * kern[5] for i in range(2)]))
     store(16, field[:N])
     store(17, field[N:])
-    return_planes((1, 3), rows=REST)
-    for k in (3, 2, 1):
+    return_planes((1, 3), (0, 3), rows=REST)
+    for k in (2, 1, 0):
+        return_planes((1, k))
         return_planes((0, k))
-        return_planes((1, k - 1))
-    return_planes((0, 0))
 
     def synthesise(k):
         mine = plane_index(x_hi, band, k, core)
@@ -336,14 +336,8 @@
             return pltpu.make_async_copy(send_b.at[mine, rows], recv_b.at[k, me, rows], b_local.at[sem])
 
         if k == 3:
-            @pl.when(lower)
-            def _():
-                mine_back(ALL, 3).wait()
-
-            @pl.when(jnp.logical_not(lower))
-            def _():
-                mine_back(FIRST, 3).wait()
-                mine_back(REST, 4).wait()
+            mine_back(FIRST, 3).wait()
+            mine_back(REST, 4).wait()
         else:
             mine_back(ALL, k).wait()
         block = recv_b.at[k, pl.ds(0, PEERS - 1), used]
@@ -376,6 +370,9 @@
                 index = (to_k, (r - back) % 8)
                 pltpu.make_async_remote_copy(part.at[k, e], inner.at[index], sum_send, inner_recv.at[index],
                                              device_id=layer(-step, to_core), device_id_type=MESH).start()
+            elif (here, r) in COLLECTED:
+                pltpu.make_async_remote_copy(part.at[k, e], inner.at[0, r], sum_send, inner_recv.at[0, r],
+                                             device_id=layer(-step, 0), device_id_type=MESH).start()
             else:
                 hand_in(k, e, r, -step, 0 if step > 0 else 1).start()
 
@@ -394,6 +391,9 @@
     @pl.when(lower)
     def _():
         for r in HELD:
+            if any(r == collected for _, collected in COLLECTED):
+                pltpu.make_async_copy(inner.at[0, r], inner.at[0, r], inner_recv.at[0, r]).wait()
+                part[0, r] += inner[0, r]
             keeps = jnp.logical_and(home == 0, rank == r)
             local = pltpu.make_async_copy(part.at[0, r], arrive.at[2, slot], arrive_recv.at[2, slot])
             pl.when(keeps)(lambda: local.start())

time: 69.4 us -> 69 us (level)
  no operation moved by 1% of the time
where the time goes in v4:
time: 69 us; the launch traced here: 68.9 us
  Pallas kernels  68.2 us (99%)
  local copies, waits for them, and re-layouts  0.71 us (1%)
    pallas_call x1, Pallas kernels, per_device(): pl.pallas_call(kernel, out_shape=jax.ShapeDtypeStruct((4 * N, N), F32), i...  68.2 us

profile of v4, /device:TPU:1, one launch (start us, length us, event | category | flops | bytes accessed | tf_op | source)
XLA Modules:
  0.0 68.9 jit_solution(377324741260864314)
XLA Ops:
  0.0 68.2 %exchange.1 = f32[512,128]{1,0:T(8,128)S(1)} custom-call(f32[512,128]{1,0:T(8,128)} %bitcast.3, bf16[12,256,256]{2,1,0:T(8,128)(2,1)} %constant.2.clone.tables), custom_call_target="tpu_custom_call" | custom-call | tf_op jit(solution)/shard_map/exchange/pallas_call | solution.py:432
  68.2 0.7 %copy.4 = f32[1,4,128,128]{3,2,1,0:T(8,128)} copy(f32[1,4,128,128]{3,2,1,0:T(8,128)S(1)} %bitcast.2) | data formatting | bytes 524288

commit v5 on v4

--- a/solution.py
+++ b/solution.py
@@ -12,7 +12,7 @@
 PEERS = 32
 USED, PITCH = 18, 24
 BF16, F32 = jnp.bfloat16, jnp.float32
-COLLECTED = ((2, 3), (6, 1))
+COLLECTED = ((2, 3), (6, 1), (2, 6), (6, 6))
 ALL, FIRST, REST = (0, USED), (0, 8), (8, USED - 8)
 ORDER = [(2, 2), (1, 1), (3, 3), (2, 1), (3, 1), (1, 3), (2, 3), (1, 2), (3, 2), (1, 0), (0, 3), (3, 0), (0, 1), (2, 0), (0, 2)]
 FWD, INV, Y_FWD, Y_INV, HALF_FWD, HALF_INV = range(6)
@@ -49,6 +49,8 @@
 
 
 def sides(r):
+    if r == 6:
+        return [0]
     strides = [stride_of(0, end) for end in starts_at(0, r) if (end, r) not in COLLECTED]
     return [side for side, present in enumerate((max(strides) > 0, min(strides) < 0, r in HELD)) if present]
 
@@ -371,8 +373,9 @@
                 pltpu.make_async_remote_copy(part.at[k, e], inner.at[index], sum_send, inner_recv.at[index],
                                              device_id=layer(-step, to_core), device_id_type=MESH).start()
             elif (here, r) in COLLECTED:
-                pltpu.make_async_remote_copy(part.at[k, e], inner.at[0, r], sum_send, inner_recv.at[0, r],
-                                             device_id=layer(-step, 0), device_id_type=MESH).start()
+                index = (0, 7 if r == 6 and step < 0 else r)
+                pltpu.make_async_remote_copy(part.at[k, e], inner.at[index], sum_send, inner_recv.at[index],
+                                             device_id=layer(-step, source_core(r)), device_id_type=MESH).start()
             else:
                 hand_in(k, e, r, -step, 0 if step > 0 else 1).start()
 
@@ -382,11 +385,23 @@
             part.at[k, e], arrive.at[side, slot], sum_send, arrive_recv.at[side, slot],
             device_id=at(lax.rem(to_z + r, 8), (x_hi * 8 + to_z) * 2 + home), device_id_type=MESH)
 
+    kept_six = jnp.logical_and(home == 1, rank == 6)
+
+    def join_sums():
+        for e in (6, 7):
+            pltpu.make_async_copy(inner.at[0, e], inner.at[0, e], inner_recv.at[0, e]).wait()
+        part[0, 6] = inner[0, 6] + inner[0, 7]
+        local = pltpu.make_async_copy(part.at[0, 6], arrive.at[0, slot], arrive_recv.at[0, slot])
+        pl.when(kept_six)(lambda: local.start())
+        pl.when(jnp.logical_not(kept_six))(lambda: hand_in(0, 6, 6, 0, 0).start())
+
     for k in (3, 2, 1, 0):
         synthesise(k)
         if k:
             pl.when(lower)(lambda k=k: pass_sums(0, k))
         pl.when(jnp.logical_not(lower))(lambda k=k: pass_sums(1, k))
+        if k == 1:
+            pl.when(jnp.logical_not(lower))(join_sums)
 
     @pl.when(lower)
     def _():
@@ -421,8 +436,10 @@
     pl.when(lower)(lambda: left_by(relay_send, vis, 13))
     pl.when(jnp.logical_not(lower))(lambda: left_by(relay_send, vis, 15))
     kept = jnp.logical_and(jnp.logical_and(lower, home == 0), in_held == 1)
+    sixteen = jnp.logical_or(jnp.logical_and(lower, jnp.logical_not(kept)), jnp.logical_and(jnp.logical_not(lower), kept_six))
     pl.when(kept)(lambda: left_by(sum_send, part, 15))
-    pl.when(jnp.logical_not(kept))(lambda: left_by(sum_send, part, 16))
+    pl.when(sixteen)(lambda: left_by(sum_send, part, 16))
+    pl.when(jnp.logical_and(jnp.logical_not(lower), jnp.logical_not(kept_six)))(lambda: left_by(sum_send, part, 17))
 
 
 def per_device(wavefunctions, tables):

time: 69 us -> 71.5 us (1.036)
  Pallas kernels: 68.2 us -> 70.7 us
    pallas_call x1, Pallas kernels: 68.2 us -> 70.7 us  [per_device(): pl.pallas_call(kernel, out_shape=jax.ShapeDtypeStruct((4 * N, N), F32), i...]
where the time goes in v5:
time: 71.5 us; the launch traced here: 71.4 us
  Pallas kernels  70.7 us (99%)
    pallas_call x1, Pallas kernels, per_device(): pl.pallas_call(kernel, out_shape=jax.ShapeDtypeStruct((4 * N, N), F32), i...  70.7 us

profile of v5, /device:TPU:1, one launch (start us, length us, event | category | flops | bytes accessed | tf_op | source)
XLA Modules:
  0.0 71.4 jit_solution(5955481361694195692)
XLA Ops:
  0.0 70.7 %exchange.1 = f32[512,128]{1,0:T(8,128)S(1)} custom-call(f32[512,128]{1,0:T(8,128)} %bitcast.3, bf16[12,256,256]{2,1,0:T(8,128)(2,1)} %constant.2.clone.tables), custom_call_target="tpu_custom_call" | custom-call | tf_op jit(solution)/shard_map/exchange/pallas_call | solution.py:449
  70.7 0.7 copy.4
